TPU v7x, 32 devices: a whole 2x2x4 slice. The times are simulated.
32 devices in a mesh: shot: 16 (over z, x, core), depth: 2 (over y).
Axes of the slice: x: 2, y: 2, z: 4, core: 2. Of those that a mesh axis runs over, the one named last changes fastest.
Arguments:
- u_prev: float32 [16, 64, 32, 128], P('shot', None, 'depth'), may hold values from -8 to 8.5
- u_cur: float32 [16, 64, 32, 128], P('shot', None, 'depth'), may hold values from -8 to 8.5
- a_prev: float32 [16, 64, 32, 128], P('shot', None, 'depth'), may hold values from -8 to 8.5
- a_cur: float32 [16, 64, 32, 128], P('shot', None, 'depth'), may hold values from -8 to 8.5
- model: float32 [64, 32, 128], P('shot', 'depth'), may hold values from 0.03 to 0.09
- aniso_h: float32 [64, 32, 128], P('shot', 'depth'), may hold values from 0.7 to 1.5
- aniso_c: float32 [64, 32, 128], P('shot', 'depth'), may hold values from -0.5 to 0.5
- smooth_coef: float32 [64, 32, 128], P('shot', 'depth'), may hold values from 0.02 to 0.16
- bin_onehot: int32 [16, 4, 4], P(None, 'depth'), may hold values from 0 to 1, as said below
- shot_group: int32 [16], P('shot'), may hold values from 0 to 15
- src_cell: int32 [16], P('shot'), may hold values from 0 to 262143
- rec_cell: int32 [16, 128], P('shot'), may hold values from 0 to 262143
- src_wave: float32 [16, 3], P('shot'), may hold values from -6 to 6
- rec_data: float32 [16, 2, 128], P('shot'), may hold values from -6 to 6
Outputs:
- model_next: float32 [64, 32, 128], P('shot', 'depth')
- grad_dir: float32 [64, 32, 128], P('shot', 'depth')
- wave_next: float32 [16, 64, 32, 128], P('shot', None, 'depth')
Inputs may be any that keep to these rules, and one draw needn't show every extreme that they name: `bin_onehot`: each entry along the last dimension is one-hot: exactly one 1 per row.
All inputs are finite; a program needn't handle non-finite values.
Results may differ from a plain program's by a relative error of at most 0.000092.
Values sent between devices are 32-bit elements; how exact they have to be, the bound alone decides.
A program may use at most 64 MiB of HBM per device.

v0:
```python
import jax
import jax.numpy as jnp
from jax import lax
from jax.sharding import PartitionSpec as P

second_coef = (-205.0 / 72.0, 8.0 / 5.0, -1.0 / 5.0, 8.0 / 315.0, -1.0 / 560.0)
first_coef = (0.8, -0.2, 4.0 / 105.0, -1.0 / 280.0)


def extended(block, sides, width):
    for axis, dim in sides:
        count = lax.axis_size(axis)
        forward = [(i, i + 1) for i in range(count - 1)]
        backward = [(target, source) for source, target in forward]
        low = lax.ppermute(
            lax.slice_in_dim(block, block.shape[dim] - width, None, axis=dim), axis, forward
        )
        high = lax.ppermute(lax.slice_in_dim(block, 0, width, axis=dim), axis, backward)
        block = jnp.concatenate([low, block, high], axis=dim)
    return block


def pad_axis(field, axis, width):
    widths = [(0, 0)] * field.ndim
    widths[axis] = (width, width)
    return jnp.pad(field, widths)


def shifted(padded, axis, offset, count):
    return lax.slice_in_dim(padded, 4 + offset, 4 + offset + count, axis=axis)


def second_along(padded, axis, count):
    result = second_coef[0] * shifted(padded, axis, 0, count)
    for offset in range(1, 5):
        result = result + second_coef[offset] * (
            shifted(padded, axis, offset, count) + shifted(padded, axis, -offset, count)
        )
    return result


def first_along(padded, axis, count):
    result = first_coef[0] * (shifted(padded, axis, 1, count) - shifted(padded, axis, -1, count))
    for offset in range(2, 5):
        result = result + first_coef[offset - 1] * (
            shifted(padded, axis, offset, count) - shifted(padded, axis, -offset, count)
        )
    return result


def apply_operator(padded_z, aniso_h, aniso_c):
    ndim = padded_z.ndim
    axis_x, axis_z, axis_y = (ndim - 3, ndim - 2, ndim - 1)
    count_z = padded_z.shape[axis_z] - 8
    count_x = padded_z.shape[axis_x]
    count_y = padded_z.shape[axis_y]
    centre = lax.slice_in_dim(padded_z, 4, 4 + count_z, axis=axis_z)
    depth_two = second_along(padded_z, axis_z, count_z)
    depth_one = first_along(padded_z, axis_z, count_z)
    lateral = second_along(pad_axis(centre, axis_x, 4), axis_x, count_x) + second_along(
        pad_axis(centre, axis_y, 4), axis_y, count_y
    )
    crossing = first_along(pad_axis(depth_one, axis_x, 4), axis_x, count_x)
    return aniso_h * lateral + depth_two + aniso_c * crossing


def relax_once(padded, centre, coef):
    neighbours = padded[2:, 1:-1, 1:-1] + padded[:-2, 1:-1, 1:-1]
    neighbours = neighbours + padded[1:-1, 2:, 1:-1] + padded[1:-1, :-2, 1:-1]
    neighbours = neighbours + padded[1:-1, 1:-1, 2:] + padded[1:-1, 1:-1, :-2]
    return centre + coef * (neighbours - 6.0 * centre)


def body(
    u_prev,
    u_cur,
    a_prev,
    a_cur,
    model,
    aniso_h,
    aniso_c,
    smooth_coef,
    bin_onehot,
    shot_group,
    src_cell,
    rec_cell,
    src_wave,
    rec_data,
):
    shot_count, cells_x, cells_z, cells_y = u_cur.shape
    depth_cells = cells_z * lax.axis_size("depth")
    z_start = lax.axis_index("depth") * cells_z
    model_slab, aniso_hs, aniso_cs, coef_slab = (
        lax.all_gather(model, "shot", axis=0, tiled=True),
        lax.all_gather(aniso_h, "shot", axis=0, tiled=True),
        lax.all_gather(aniso_c, "shot", axis=0, tiled=True),
        lax.all_gather(smooth_coef, "shot", axis=0, tiled=True),
    )
    x_pos = lax.broadcasted_iota(jnp.int32, (cells_x, cells_z, cells_y), 0)
    z_pos = lax.broadcasted_iota(jnp.int32, (cells_x, cells_z, cells_y), 1) + z_start
    y_pos = lax.broadcasted_iota(jnp.int32, (cells_x, cells_z, cells_y), 2)
    source_x = src_cell // (depth_cells * cells_y)
    source_z = src_cell // cells_y % depth_cells
    source_y = src_cell % cells_y
    receiver_x = rec_cell // (depth_cells * cells_y)
    receiver_z = rec_cell // cells_y % depth_cells
    receiver_y = rec_cell % cells_y
    receivers = rec_cell.shape[1]

    def source_term(step_index):
        hits = (
            (x_pos == source_x[:, None, None, None])
            & (z_pos == source_z[:, None, None, None])
            & (y_pos == source_y[:, None, None, None])
        )
        return jnp.where(hits, src_wave[:, step_index][:, None, None, None], 0.0)

    wave_pair = jnp.stack([u_cur, a_cur])
    old_pair = jnp.stack([u_prev, a_prev])
    gradient = jnp.zeros_like(u_cur)
    for step_index in range(rec_data.shape[1]):
        padded = extended(wave_pair, (("depth", 3),), 4)
        applied = apply_operator(padded, aniso_hs, aniso_cs)
        gradient = gradient + wave_pair[1] * applied[0]
        records = rec_data[:, step_index]
        along_x = (receiver_x[..., None] == jnp.arange(cells_x, dtype=jnp.int32)).astype(
            jnp.float32
        ) * records[..., None]
        along_z = (receiver_z[..., None] == z_start + jnp.arange(cells_z, dtype=jnp.int32)).astype(
            jnp.float32
        )
        along_y = (receiver_y[..., None] == jnp.arange(cells_y, dtype=jnp.int32)).astype(
            jnp.float32
        )
        plane = (along_x[..., :, None] * along_z[..., None, :]).reshape(
            shot_count, receivers, cells_x * cells_z
        )
        placed = jnp.einsum("srk,sry->sky", plane, along_y, precision=lax.Precision.HIGHEST)
        forcing = jnp.stack(
            [source_term(step_index), placed.reshape(shot_count, cells_x, cells_z, cells_y)]
        )
        next_pair = 2.0 * wave_pair - old_pair + model_slab * applied + forcing
        old_pair, wave_pair = (wave_pair, next_pair)
    nbins = bin_onehot.shape[2]
    groups = bin_onehot.shape[0]
    powers = jnp.exp2(-jnp.arange(nbins, dtype=jnp.float32))
    block_weight = jnp.sum(bin_onehot.astype(jnp.float32) * powers, axis=2)
    chosen = (shot_group[:, None] == jnp.arange(groups, dtype=jnp.int32)).astype(jnp.float32)
    shot_weight = jnp.dot(chosen, block_weight, precision=lax.Precision.HIGHEST)
    depth_weight = jnp.repeat(shot_weight, cells_z // bin_onehot.shape[1], axis=1)
    local_sum = jnp.sum(depth_weight[:, None, :, None] * gradient, axis=0)
    total_cells = cells_x * depth_cells * cells_y
    smoothed = lax.psum(local_sum, "shot")
    for sweep_index in range(2):
        rim_field = extended(smoothed, (("depth", 1),), 1)
        rim_field = pad_axis(pad_axis(rim_field, 0, 1), 2, 1)
        smoothed = relax_once(rim_field, smoothed, coef_slab)
    square_sum = lax.psum(jnp.sum(smoothed * smoothed), "depth")
    norm_scale = jnp.sqrt(square_sum / total_cells + 1e-06)
    normed_full = smoothed / norm_scale
    model_full = model_slab * (1.0 - 0.25 * jnp.tanh(normed_full))
    owner_rows = model.shape[0]
    row_start = lax.axis_index("shot") * owner_rows
    grad_dir = lax.dynamic_slice_in_dim(normed_full, row_start, owner_rows, 0)
    model_next = lax.dynamic_slice_in_dim(model_full, row_start, owner_rows, 0)
    final_padded = extended(wave_pair[0], (("depth", 2),), 4)
    final_applied = apply_operator(final_padded, aniso_hs, aniso_cs)
    wave_next = (
        2.0 * wave_pair[0]
        - old_pair[0]
        + model_full * final_applied
        + source_term(rec_data.shape[1])
    )
    return (model_next, grad_dir, wave_next)


def solution(mesh):
    return jax.shard_map(
        body,
        mesh=mesh,
        in_specs=(
            P("shot", None, "depth", None),
            P("shot", None, "depth", None),
            P("shot", None, "depth", None),
            P("shot", None, "depth", None),
            P("shot", "depth", None),
            P("shot", "depth", None),
            P("shot", "depth", None),
            P("shot", "depth", None),
            P(None, "depth", None),
            P("shot"),
            P("shot"),
            P("shot", None),
            P("shot", None),
            P("shot", None, None),
        ),
        out_specs=(
            P("shot", "depth", None),
            P("shot", "depth", None),
            P("shot", None, "depth", None),
        ),
        check_vma=False,
    )
```

profile of v0, /device:TPU:0, one launch (start us, length us, event | category | flops | bytes accessed | tf_op | source)
XLA Modules:
  0.0 267.9 jit_solution(3902824880416327258)
XLA Ops:
  7.2 0.0 all-reduce.15.cloned.1.call-start
  7.3 1.3 fusion.172
  8.6 0.0 copy-start.12
  8.6 1.3 collective-permute-start
  9.9 4.9 %collective-permute-start.1 = (f32[2,1,64,4,128]{4,3,2,1,0:T(4,128)S(1)}, f32[2,1,64,4,128]{4,3,2,1,0:T(4,128)S(1)}, u32[]{:S(2)}, u32[]{:S(2)}) collective-permute-start(f32[2,1,64,4,128]{4,3,2,1,0:T(4,128)S(1)} %get-tuple-element.15), channel_id=1, source_target_pairs={{0,1},{2,3},{4,5},{6,7},{8,9},{10,11},{12,13},{14,15},{16,17},{18,... | collective-permute-start | bytes 786440 | tf_op jit(solution)/shard_map/ppermute | solution.py:15
  15.6 0.0 copy-start.13
  15.6 1.1 pad_maximum_fusion
  16.6 0.6 fusion.197
  17.3 24.4 %all_gather.12 = f32[64,16,128]{2,1,0:T(8,128)S(1)} all-gather(f32[4,16,128]{2,1,0:T(8,128)S(1)} %copy-done.11), channel_id=1, replica_groups=mesh['shot'=16,'depth'=2] {'shot'}, dimensions={0}, use_global_device_ids=true | all-gather | bytes 557056 | tf_op jit(solution)/shard_map/all_gather | solution.py:94
  41.7 18.9 %all_gather.13 = f32[64,16,128]{2,1,0:T(8,128)S(1)} all-gather(f32[4,16,128]{2,1,0:T(8,128)S(1)} %copy-done.12), channel_id=1, replica_groups=mesh['shot'=16,'depth'=2] {'shot'}, dimensions={0}, use_global_device_ids=true | all-gather | bytes 557056 | tf_op jit(solution)/shard_map/all_gather | solution.py:95
  60.5 20.3 %all_gather.14 = f32[64,16,128]{2,1,0:T(8,128)S(1)} all-gather(f32[4,16,128]{2,1,0:T(8,128)S(1)} %copy-done.13), channel_id=1, replica_groups=mesh['shot'=16,'depth'=2] {'shot'}, dimensions={0}, use_global_device_ids=true | all-gather | bytes 557056 | tf_op jit(solution)/shard_map/all_gather | solution.py:96
  80.9 0.1 compare_convert_fusion
  80.9 0.4 convolution_bitcast_fusion.1
  81.4 1.2 convolution_bitcast_fusion
  82.6 0.1 multiply_reduce_fusion.1
  83.4 2.2 fusion.171
  85.5 0.0 collective-permute-done
  85.5 0.0 collective-permute-done.1
  85.5 0.3 pad_maximum_fusion.1
  85.8 0.0 copy-start.9
  85.8 0.0 copy-start.10
  85.9 0.8 multiply_add_fusion.1
  86.7 0.3 copy-done.5
  87.0 0.1 copy-done.9
  87.2 0.2 copy-done.10
  87.3 4.6 %fusion.87 = (f32[2,1,64,16,128]{4,3,2,1,0:T(8,128)S(1)}, f32[2,1,64,16,128]{4,3,2,1,0:T(8,128)}) fusion(f32[1,1,64,16,128]{4,3,2,1,0:T(8,128)S(1)} %bitcast.90, f32[1,1,64,16,128]{4,3,2,1,0:T(8,128)S(1)} %bitcast.91, f32[1,1,64,16,128]{4,3,2,1,0:T(8,128)S(1)} %convolution_bitcast_fusion.1, f32[1,1,64,16,128]{4,3,2,1,0:T(8,128)S(1)} %get-tuple-element.27, ...), kind=kLoop, calls=%fused_computation.182 | loop fusion | flops 15990784 | bytes 17301504 | tf_op jit(solution)/shard_map/add | solution.py:142
  92.0 0.9 fusion.193
  92.9 1.3 collective-permute-start.2
  94.1 5.3 %collective-permute-start.3 = (f32[2,1,64,4,128]{4,3,2,1,0:T(4,128)}, f32[2,1,64,4,128]{4,3,2,1,0:T(4,128)}, u32[]{:S(2)}, u32[]{:S(2)}) collective-permute-start(f32[2,1,64,4,128]{4,3,2,1,0:T(4,128)} %get-tuple-element.10), channel_id=1, source_target_pairs={{0,1},{2,3},{4,5},{6,7},{8,9},{10,11},{12,13},{14,15},{16,17},{18,... | collective-permute-start | bytes 786440 | tf_op jit(solution)/shard_map/ppermute | solution.py:15
  99.4 0.1 convolution_bitcast_fusion.2
  99.5 0.1 broadcast_in_dim.46
  99.6 0.1 broadcast_in_dim.47
  99.7 20.1 %all_gather.15 = f32[64,16,128]{2,1,0:T(8,128)} all-gather(f32[4,16,128]{2,1,0:T(8,128)S(1)} %copy-done.14), channel_id=1, replica_groups=mesh['shot'=16,'depth'=2] {'shot'}, dimensions={0}, use_global_device_ids=true | all-gather | bytes 557056 | tf_op jit(solution)/shard_map/all_gather | solution.py:97
  119.8 0.0 collective-permute-done.2
  119.8 0.0 collective-permute-done.3
  119.8 2.9 %multiply_add_fusion = f32[2,1,64,16,128]{4,3,2,1,0:T(8,128)S(1)} fusion(f32[2,1,64,4,128]{4,3,2,1,0:T(4,128)S(1)} %collective-permute-done.2, f32[2,1,64,16,128]{4,3,2,1,0:T(8,128)S(1)} %get-tuple-element.8, f32[2,1,64,4,128]{4,3,2,1,0:T(4,128)} %collective-permute-done.3), kind=kLoop, calls=%fused_computation.183 | loop fusion | flops 4980736 | bytes 2621440 | tf_op jit(solution)/shard_map/add | solution.py:45
  122.7 5.4 %fusion.37 = f32[2,1,64,16,128]{4,3,2,1,0:T(8,128)S(1)} fusion(f32[2,1,64,16,128]{4,3,2,1,0:T(8,128)S(1)} %get-tuple-element.8, f32[2,1,64,16,128]{4,3,2,1,0:T(8,128)S(1)} %multiply_add_fusion, f32[2,1,64,4,128]{4,3,2,1,0:T(4,128)S(1)} %collective-permute-done.2, f32[2,1,64,4,128]{4,3,2,1,0:T(4,128)} %collective-permute-done.3, ...), kind=kLoop, calls=%fused_computation.129 | loop fusion | flops 15990784 | bytes 4718592 | tf_op jit(solution)/shard_map/add | solution.py:64
  128.1 1.0 copy-done.6
  129.1 1.0 fusion.160
  130.0 0.0 all-reduce.15.cloned.1.call-update
  130.1 2.3 fusion.130
  132.4 85.6 %all-reduce.15.cloned.1.call-done = f32[64,16,128]{2,1,0:T(8,128)} async-done(((f32[64,16,128]{2,1,0:T(8,128)}), f32[64,16,128]{2,1,0:T(8,128)}) %all-reduce.15.cloned.1.call-update) | async-done | bytes 524304 | tf_op jit(solution)/shard_map/psum | solution.py:153
  218.0 1.2 fusion.195
  219.2 3.4 %collective-permute-start.4 = (f32[64,1,128]{2,1,0:T(1,128)S(1)}, f32[64,1,128]{2,1,0:T(1,128)S(1)}, u32[]{:S(2)}, u32[]{:S(2)}) collective-permute-start(f32[64,1,128]{2,1,0:T(1,128)S(1)} %get-tuple-element.18), channel_id=1, source_target_pairs={{0,1},{2,3},{4,5},{6,7},{8,9},{10,11},{12,13},{14,15},{16,17},{18,... | collective-permute-start | bytes 98312 | tf_op jit(solution)/shard_map/ppermute | solution.py:15
  222.6 1.3 collective-permute-start.5
  223.9 1.1 fusion.196
  225.0 1.3 collective-permute-start.8
  226.3 4.6 %collective-permute-start.9 = (f32[1,64,4,128]{3,2,1,0:T(4,128)S(1)}, f32[1,64,4,128]{3,2,1,0:T(4,128)S(1)}, u32[]{:S(2)}, u32[]{:S(2)}) collective-permute-start(f32[1,64,4,128]{3,2,1,0:T(4,128)S(1)} %get-tuple-element.20), channel_id=1, source_target_pairs={{0,1},{2,3},{4,5},{6,7},{8,9},{10,11},{12,13},{14,15},{16,17},{18,... | collective-permute-start | bytes 393224 | tf_op jit(solution)/shard_map/ppermute | solution.py:15
  230.8 0.0 collective-permute-done.4
  230.8 0.0 collective-permute-done.5
  230.8 1.2 select_maximum_fusion.2
  232.0 0.5 fusion.135
  232.6 1.3 collective-permute-start.6
  233.9 1.3 collective-permute-start.7
  235.2 0.0 collective-permute-done.8
  235.2 0.0 collective-permute-done.9
  235.2 1.5 multiply_add_fusion.2
  236.7 0.0 collective-permute-done.6
  236.7 3.0 %collective-permute-done.7 = f32[64,1,128]{2,1,0:T(1,128)S(1)} collective-permute-done((f32[64,1,128]{2,1,0:T(1,128)S(1)}, f32[64,1,128]{2,1,0:T(1,128)S(1)}, u32[]{:S(2)}, u32[]{:S(2)}) %collective-permute-start.7) | collective-permute-done | bytes 32800 | tf_op jit(solution)/shard_map/ppermute | solution.py:18
  239.7 0.1 select_maximum_fusion
  239.8 1.9 multiply_reduce_fusion
  241.7 5.5 %psum.15 = f32[]{:T(128)} all-reduce(f32[]{:T(128)} %get-tuple-element.6), channel_id=1, replica_groups=mesh['shot'=16,'depth'=2] {'depth'}, use_global_device_ids=true, to_apply=%region_3.4 | all-reduce | flops 1 | bytes 8 | tf_op jit(solution)/shard_map/psum | solution.py:158
  248.0 12.4 %fusion.101 = (f32[1,64,16,128]{3,2,1,0:T(8,128)}, f32[64,16,128]{2,1,0:T(8,128)S(1)}, f32[64,16,128]{2,1,0:T(8,128)S(1)}) fusion(f32[1,64,16,128]{3,2,1,0:T(8,128)} %fusion.130, f32[1,64,16,128]{3,2,1,0:T(8,128)} %multiply_add_fusion.2, f32[64,16,128]{2,1,0:T(8,128)S(1)} %all_gather.14, f32[64,16,128]{2,1,0:T(8,128)S(1)} %all_gather.13, ...), kind=kLoop, calls=%fused_computation.224 | loop fusion | flops 9830400 | bytes 5505056 | tf_op jit(solution)/shard_map/add | solution.py:169
  260.4 0.6 constant_dynamic-slice_fusion
  (37 shorter events, 0.2 us)
Async XLA Ops:
  7.2 8.4 %copy-start.1 = (f32[1,64,16,128]{3,2,1,0:T(8,128)S(1)}, f32[1,64,16,128]{3,2,1,0:T(8,128)}, u32[]{:S(2)}) copy-start(f32[1,64,16,128]{3,2,1,0:T(8,128)} %param.15) | copy-start | bytes 1572868
  7.2 8.4 %copy-start = (f32[1,64,16,128]{3,2,1,0:T(8,128)S(1)}, f32[1,64,16,128]{3,2,1,0:T(8,128)}, u32[]{:S(2)}) copy-start(f32[1,64,16,128]{3,2,1,0:T(8,128)} %param.17) | copy-start | bytes 1572868
  7.2 210.8 %all-reduce.15.cloned.1.call-start = ((), (), s32[]{:S(2)}) async-start(), calls=%async_computation | async-start | bytes 1048576 | tf_op jit(solution)/shard_map/psum | solution.py:153
  7.2 9.4 %copy-start.15 = (f32[1,3]{1,0:T(1,128)S(1)}, f32[1,3]{1,0:T(1,128)}, u32[]{:S(2)}) copy-start(f32[1,3]{1,0:T(1,128)} %param.26) | copy-start | bytes 40
  7.2 10.0 %copy-start.18 = (s32[1,128]{1,0:T(1,128)S(1)}, s32[1,128]{1,0:T(1,128)}, u32[]{:S(2)}) copy-start(s32[1,128]{1,0:T(1,128)} %param.25) | copy-start | bytes 1540
  7.3 10.0 %copy-start.17 = (f32[1,2,128]{2,1,0:T(2,128)S(1)}, f32[1,2,128]{2,1,0:T(2,128)}, u32[]{:S(2)}) copy-start(f32[1,2,128]{2,1,0:T(2,128)} %param.27) | copy-start | bytes 3076
  7.3 10.0 %copy-start.11 = (f32[4,16,128]{2,1,0:T(8,128)S(1)}, f32[4,16,128]{2,1,0:T(8,128)}, u32[]{:S(2)}) copy-start(f32[4,16,128]{2,1,0:T(8,128)} %param.18) | copy-start | bytes 98308
  8.6 33.0 %copy-start.12 = (f32[4,16,128]{2,1,0:T(8,128)S(1)}, f32[4,16,128]{2,1,0:T(8,128)}, u32[]{:S(2)}) copy-start(f32[4,16,128]{2,1,0:T(8,128)} %param.19) | copy-start | bytes 98308
  8.6 76.9 %collective-permute-start = (f32[2,1,64,4,128]{4,3,2,1,0:T(4,128)S(1)}, f32[2,1,64,4,128]{4,3,2,1,0:T(4,128)S(1)}, u32[]{:S(2)}, u32[]{:S(2)}) collective-permute-start(f32[2,1,64,4,128]{4,3,2,1,0:T(4,128)S(1)} %get-tuple-element.14), channel_id=1, source_target_pairs={{1,0},{3,2},{5,4},{7,6},{9,8},{11,10},{13,12},{15,14},{17,16},{19,... | collective-permute-start | bytes 786440 | tf_op jit(solution)/shard_map/ppermute | solution.py:18
  9.9 75.6 %collective-permute-start.1 = (f32[2,1,64,4,128]{4,3,2,1,0:T(4,128)S(1)}, f32[2,1,64,4,128]{4,3,2,1,0:T(4,128)S(1)}, u32[]{:S(2)}, u32[]{:S(2)}) collective-permute-start(f32[2,1,64,4,128]{4,3,2,1,0:T(4,128)S(1)} %get-tuple-element.15), channel_id=1, source_target_pairs={{0,1},{2,3},{4,5},{6,7},{8,9},{10,11},{12,13},{14,15},{16,17},{18,... | collective-permute-start | bytes 786440 | tf_op jit(solution)/shard_map/ppermute | solution.py:15
  15.6 45.0 %copy-start.13 = (f32[4,16,128]{2,1,0:T(8,128)S(1)}, f32[4,16,128]{2,1,0:T(8,128)}, u32[]{:S(2)}) copy-start(f32[4,16,128]{2,1,0:T(8,128)} %param.20) | copy-start | bytes 98308
  16.6 66.0 %copy-start.16 = (s32[16,2,4]{0,2,1:T(4,128)S(1)}, s32[16,2,4]{0,2,1:T(4,128)}, u32[]{:S(2)}) copy-start(s32[16,2,4]{0,2,1:T(4,128)} %param.22) | copy-start | bytes 1540
  41.7 45.1 %copy-start.2 = (f32[64,16,128]{2,1,0:T(8,128)}, f32[64,16,128]{2,1,0:T(8,128)S(1)}, u32[]{:S(2)}) copy-start(f32[64,16,128]{2,1,0:T(8,128)S(1)} %all_gather.12) | copy-start | bytes 1572868
  85.8 1.2 copy-start.5
  85.8 1.3 copy-start.9
  85.8 1.5 copy-start.10
  87.3 12.4 %copy-start.14 = (f32[4,16,128]{2,1,0:T(8,128)S(1)}, f32[4,16,128]{2,1,0:T(8,128)}, u32[]{:S(2)}) copy-start(f32[4,16,128]{2,1,0:T(8,128)} %param.21) | copy-start | bytes 98308
  92.9 27.0 %collective-permute-start.2 = (f32[2,1,64,4,128]{4,3,2,1,0:T(4,128)}, f32[2,1,64,4,128]{4,3,2,1,0:T(4,128)S(1)}, u32[]{:S(2)}, u32[]{:S(2)}) collective-permute-start(f32[2,1,64,4,128]{4,3,2,1,0:T(4,128)} %get-tuple-element.11), channel_id=1, source_target_pairs={{1,0},{3,2},{5,4},{7,6},{9,8},{11,10},{13,12},{15,14},{17,16},{19,... | collective-permute-start | bytes 786440 | tf_op jit(solution)/shard_map/ppermute | solution.py:18
  94.1 25.7 %collective-permute-start.3 = (f32[2,1,64,4,128]{4,3,2,1,0:T(4,128)}, f32[2,1,64,4,128]{4,3,2,1,0:T(4,128)}, u32[]{:S(2)}, u32[]{:S(2)}) collective-permute-start(f32[2,1,64,4,128]{4,3,2,1,0:T(4,128)} %get-tuple-element.10), channel_id=1, source_target_pairs={{0,1},{2,3},{4,5},{6,7},{8,9},{10,11},{12,13},{14,15},{16,17},{18,... | collective-permute-start | bytes 786440 | tf_op jit(solution)/shard_map/ppermute | solution.py:15
  122.7 6.4 %copy-start.8 = (f32[2,1,64,16,128]{4,3,2,1,0:T(8,128)S(1)}, f32[2,1,64,16,128]{4,3,2,1,0:T(8,128)}, u32[]{:S(2)}) copy-start(f32[2,1,64,16,128]{4,3,2,1,0:T(8,128)} %get-tuple-element.9) | copy-start | bytes 3145732
  128.1 1.0 copy-start.6
  218.0 14.0 %copy-start.4 = (f32[64,16,128]{2,1,0:T(8,128)S(1)}, f32[64,16,128]{2,1,0:T(8,128)}, u32[]{:S(2)}) copy-start(f32[64,16,128]{2,1,0:T(8,128)} %all_gather.15) | copy-start | bytes 1572868
  218.0 14.0 %copy-start.7 = (f32[64,16,128]{2,1,0:T(8,128)S(1)}, f32[64,16,128]{2,1,0:T(8,128)}, u32[]{:S(2)}) copy-start(f32[64,16,128]{2,1,0:T(8,128)} %all-reduce.15.cloned.1.call-done) | copy-start | bytes 1572868
  219.2 11.6 %collective-permute-start.4 = (f32[64,1,128]{2,1,0:T(1,128)S(1)}, f32[64,1,128]{2,1,0:T(1,128)S(1)}, u32[]{:S(2)}, u32[]{:S(2)}) collective-permute-start(f32[64,1,128]{2,1,0:T(1,128)S(1)} %get-tuple-element.18), channel_id=1, source_target_pairs={{0,1},{2,3},{4,5},{6,7},{8,9},{10,11},{12,13},{14,15},{16,17},{18,... | collective-permute-start | bytes 98312 | tf_op jit(solution)/shard_map/ppermute | solution.py:15
  222.6 8.3 %collective-permute-start.5 = (f32[64,1,128]{2,1,0:T(1,128)S(1)}, f32[64,1,128]{2,1,0:T(1,128)S(1)}, u32[]{:S(2)}, u32[]{:S(2)}) collective-permute-start(f32[64,1,128]{2,1,0:T(1,128)S(1)} %get-tuple-element.19), channel_id=1, source_target_pairs={{1,0},{3,2},{5,4},{7,6},{9,8},{11,10},{13,12},{15,14},{17,16},{19,... | collective-permute-start | bytes 98312 | tf_op jit(solution)/shard_map/ppermute | solution.py:18
  225.0 10.2 %collective-permute-start.8 = (f32[1,64,4,128]{3,2,1,0:T(4,128)S(1)}, f32[1,64,4,128]{3,2,1,0:T(4,128)S(1)}, u32[]{:S(2)}, u32[]{:S(2)}) collective-permute-start(f32[1,64,4,128]{3,2,1,0:T(4,128)S(1)} %get-tuple-element.21), channel_id=1, source_target_pairs={{1,0},{3,2},{5,4},{7,6},{9,8},{11,10},{13,12},{15,14},{17,16},{19,... | collective-permute-start | bytes 393224 | tf_op jit(solution)/shard_map/ppermute | solution.py:18
  226.3 8.9 %collective-permute-start.9 = (f32[1,64,4,128]{3,2,1,0:T(4,128)S(1)}, f32[1,64,4,128]{3,2,1,0:T(4,128)S(1)}, u32[]{:S(2)}, u32[]{:S(2)}) collective-permute-start(f32[1,64,4,128]{3,2,1,0:T(4,128)S(1)} %get-tuple-element.20), channel_id=1, source_target_pairs={{0,1},{2,3},{4,5},{6,7},{8,9},{10,11},{12,13},{14,15},{16,17},{18,... | collective-permute-start | bytes 393224 | tf_op jit(solution)/shard_map/ppermute | solution.py:15
  232.0 3.2 %copy-start.3 = (f32[1,64,16,128]{3,2,1,0:T(8,128)S(1)}, f32[1,64,16,128]{3,2,1,0:T(8,128)}, u32[]{:S(2)}) copy-start(f32[1,64,16,128]{3,2,1,0:T(8,128)} %fusion.130) | copy-start | bytes 1572868
  232.6 4.1 %collective-permute-start.6 = (f32[64,1,128]{2,1,0:T(1,128)S(1)}, f32[64,1,128]{2,1,0:T(1,128)S(1)}, u32[]{:S(2)}, u32[]{:S(2)}) collective-permute-start(f32[64,1,128]{2,1,0:T(1,128)S(1)} %get-tuple-element.16), channel_id=1, source_target_pairs={{0,1},{2,3},{4,5},{6,7},{8,9},{10,11},{12,13},{14,15},{16,17},{18,... | collective-permute-start | bytes 98312 | tf_op jit(solution)/shard_map/ppermute | solution.py:15
  233.9 5.8 %collective-permute-start.7 = (f32[64,1,128]{2,1,0:T(1,128)S(1)}, f32[64,1,128]{2,1,0:T(1,128)S(1)}, u32[]{:S(2)}, u32[]{:S(2)}) collective-permute-start(f32[64,1,128]{2,1,0:T(1,128)S(1)} %get-tuple-element.17), channel_id=1, source_target_pairs={{1,0},{3,2},{5,4},{7,6},{9,8},{11,10},{13,12},{15,14},{17,16},{19,... | collective-permute-start | bytes 98312 | tf_op jit(solution)/shard_map/ppermute | solution.py:18
Sparse Core Ops, SparseCore 0:
  130.2 87.7 all-reduce.14
where the time goes:
time: 269 us; the launch traced here: 268 us
  blocking collectives  89.2 us (33%)
  waiting for transfers between devices  88.7 us (33%)
  other arithmetic  39.6 us (15%)
  starting transfers between devices  25.9 us (10%)
  between operations  16.5 us (6%)
  local copies, waits for them, and re-layouts  6.2 us (2%)
    psum x1, waiting for transfers between devices, body(): smoothed = lax.psum(local_sum, 'shot')  85.6 us
    all_gather x1, blocking collectives, body(): lax.all_gather(model, 'shot', axis=0, tiled=True)  24.4 us
    all_gather x1, blocking collectives, body(): lax.all_gather(aniso_c, 'shot', axis=0, tiled=True)  20.3 us
    all_gather x1, blocking collectives, body(): lax.all_gather(smooth_coef, 'shot', axis=0, tiled=True)  20.1 us
    ppermute x5, starting transfers between devices, extended(): lax.ppermute(lax.slice_in_dim(block, block.shape[dim] - width, None, axis...  19.4 us
    all_gather x1, blocking collectives, body(): lax.all_gather(aniso_h, 'shot', axis=0, tiled=True)  18.9 us
    add x1, other arithmetic, body(): 2.0 * wave_pair[0] - old_pair[0] + model_full * final_applied  12.4 us
    ppermute x5, starting transfers between devices, extended(): lax.ppermute(lax.slice_in_dim(block, 0, width, axis=dim), axis, backward)  6.45 us
  transfers between devices with their start and end apart: 11, of which 2 were waited for; matrix products, arithmetic and copies ran while one was open for 5% of the time, Pallas kernels for 0%

commit v1 on v0

v1 whole, which is shorter than its diff:
```python
import functools

import jax
import jax.numpy as jnp
from jax import lax
from jax.experimental import pallas as pl
from jax.experimental.pallas import tpu as pltpu
from jax.sharding import PartitionSpec as P

MESH = pl.DeviceIdType.MESH
second_coef = (-205.0 / 72.0, 8.0 / 5.0, -1.0 / 5.0, 8.0 / 315.0, -1.0 / 560.0)
first_coef = (0.8, -0.2, 4.0 / 105.0, -1.0 / 280.0)
XP = 4
ZP = 8


def kernel(
    dims,
    u_prev,
    u_cur,
    a_prev,
    a_cur,
    model,
    aniso_h,
    aniso_c,
    smooth_coef,
    bins,
    shot_group,
    src_cell,
    rec_cell,
    src_wave,
    rec_data,
    model_next,
    grad_dir,
    wave_next,
    eu0,
    eu1,
    eu2,
    ea0,
    up,
    ap,
    coefs,
    eco,
    lat_u,
    dz_u,
    cr_u,
    lat_a,
    dz_a,
    cr_a,
    rec_field,
    a1,
    grad,
    half_in,
    part,
    block_in,
    es0,
    es1,
    sq,
    model_own,
    grad_own,
    load_sem,
    halo_send,
    halo_recv,
    g_send,
    g_recv,
    k_send,
    k_recv,
    s_send,
    s_recv,
    half_send,
    half_recv,
    rs_send,
    rs_recv,
    sq_send,
    sq_recv,
    out_sem,
):
    S, D, R, X, Z, Y, NB, BK = dims
    Q = S // 2
    O = Q // 2
    me = lax.axis_index("shot")
    d = lax.axis_index("depth")
    core = lax.rem(me, 2)
    chip = me // 2
    inner = lax.rem(chip, 2)
    outer = chip // 2
    ZI = slice(ZP, ZP + Z)

    def sid(o, p, c):
        return (o * 2 + p) * 2 + c

    own = pl.ds(me * R, R)
    loads = [
        pltpu.make_async_copy(model, coefs.at[0, own], load_sem.at[0]),
        pltpu.make_async_copy(aniso_h, coefs.at[1, own], load_sem.at[1]),
        pltpu.make_async_copy(aniso_c, coefs.at[2, own], load_sem.at[2]),
        pltpu.make_async_copy(smooth_coef, eco.at[own, ZI], load_sem.at[3]),
        pltpu.make_async_copy(u_cur.at[0], eu0.at[pl.ds(XP, X), ZI], load_sem.at[4]),
        pltpu.make_async_copy(a_cur.at[0], ea0.at[pl.ds(XP, X), ZI], load_sem.at[5]),
        pltpu.make_async_copy(u_prev.at[0], up, load_sem.at[6]),
        pltpu.make_async_copy(a_prev.at[0], ap, load_sem.at[7]),
    ]
    for load in loads:
        load.start()

    def zero_z(i, carry):
        for ref in (eu0, eu1, eu2, ea0, es0, es1):
            ref[i, 0:ZP, :] = jnp.zeros((ZP, Y), jnp.float32)
            ref[i, ZP + Z :, :] = jnp.zeros((ZP, Y), jnp.float32)
        return carry

    lax.fori_loop(0, X + 2 * XP, zero_z, 0)

    def zero_c(i, carry):
        eco[i, 0:ZP, :] = jnp.zeros((ZP, Y), jnp.float32)
        eco[i, ZP + Z :, :] = jnp.zeros((ZP, Y), jnp.float32)
        return carry

    lax.fori_loop(0, X, zero_c, 0)
    for ref in (eu0, eu1, eu2, ea0, es0, es1):
        for i in list(range(XP)) + list(range(XP + X, X + 2 * XP)):
            ref[i, ZI, :] = jnp.zeros((Z, Y), jnp.float32)
    for ref in (cr_u, cr_a):
        for i in list(range(XP)) + list(range(XP + X, X + 2 * XP)):
            ref[i] = jnp.zeros((Z, Y), jnp.float32)

    barrier = pltpu.get_barrier_semaphore()
    peers = [(sid(outer, inner, 1 - core), d)]
    for i in range(1, Q):
        peers.append((lax.rem(chip + i, Q) * 2 + core, d))
    for i in range(1, D):
        peers.append((me, lax.rem(d + i, D)))
    for peer in peers:
        pl.semaphore_signal(barrier, inc=1, device_id=peer, device_id_type=MESH)
    pl.semaphore_wait(barrier, len(peers))

    def remote(src, dst, ss, rs, peer):
        return pltpu.make_async_remote_copy(
            src_ref=src, dst_ref=dst, send_sem=ss, recv_sem=rs, device_id=peer, device_id_type=MESH
        )

    class Gather:
        def __init__(self, at, send, recv):
            self.at, self.send, self.recv = at, send, recv
            self.sent = []

        def go(self, s, sem, peer):
            copy = remote(self.at(s), self.at(s), self.send.at[sem], self.recv.at[sem], peer)
            copy.start()
            self.sent.append(copy)

        def landed(self, s, sem):
            ref = self.at(s)
            remote(ref, ref, self.send.at[sem], self.recv.at[sem], (me, d)).wait_recv()

        def start(self):
            for i in range(1, O):
                self.go(me, i, (sid(lax.rem(outer + i, O), inner, core), d))
            self.go(me, O, (sid(outer, 1 - inner, core), d))
            self.go(me, 2 * O, (sid(outer, inner, 1 - core), d))

        def forward_outer(self):
            for i in range(1, O):
                s = sid(lax.rem(outer + O - i, O), inner, core)
                self.landed(s, i)
                self.go(s, O + i, (sid(outer, 1 - inner, core), d))
                self.go(s, 2 * O + i, (sid(outer, inner, 1 - core), d))

        def forward_inner(self):
            for i in range(O):
                s = sid(lax.rem(outer + O - i, O), 1 - inner, core)
                self.landed(s, O + i)
                self.go(s, 3 * O + i, (sid(outer, inner, 1 - core), d))

        def finish(self):
            for i in range(O):
                self.landed(sid(lax.rem(outer + O - i, O), inner, 1 - core), 2 * O + i)
            for i in range(O):
                self.landed(sid(lax.rem(outer + O - i, O), 1 - inner, 1 - core), 3 * O + i)

        def drain(self):
            for copy in self.sent:
                copy.wait_send()

    class Halo:
        def __init__(self, ref, width, slot, rows):
            self.up = remote(
                ref.at[rows, ZP + Z - width : ZP + Z], ref.at[rows, ZP - width : ZP],
                halo_send.at[slot], halo_recv.at[slot], (me, jnp.minimum(d + 1, D - 1)),
            )
            self.down = remote(
                ref.at[rows, ZP : ZP + width], ref.at[rows, ZP + Z : ZP + Z + width],
                halo_send.at[slot + 1], halo_recv.at[slot + 1], (me, jnp.maximum(d - 1, 0)),
            )

        def start(self):
            pl.when(d < D - 1)(lambda: self.up.start())
            pl.when(d > 0)(lambda: self.down.start())

        def wait(self):
            pl.when(d > 0)(lambda: self.up.wait_recv())
            pl.when(d < D - 1)(lambda: self.down.wait_recv())

        def drain(self):
            pl.when(d < D - 1)(lambda: self.up.wait_send())
            pl.when(d > 0)(lambda: self.down.wait_send())

    rows = pl.ds(XP, X)
    for load in loads[:3]:
        load.wait()
    gather = Gather(lambda s: coefs.at[:, pl.ds(s * R, R)], g_send, g_recv)
    gather.start()
    loads[4].wait()
    halo_u0 = Halo(eu0, 4, 0, rows)
    halo_u0.start()
    loads[5].wait()
    halo_a0 = Halo(ea0, 4, 2, rows)
    halo_a0.start()
    loads[3].wait()
    gather_k = Gather(lambda s: eco.at[pl.ds(s * R, R), ZI], k_send, k_recv)
    gather_k.start()

    lane = lax.broadcasted_iota(jnp.int32, (R, Z, Y), 2)
    local_x = lax.broadcasted_iota(jnp.int32, (R, Z, Y), 0)
    local_z = lax.broadcasted_iota(jnp.int32, (R, Z, Y), 1)
    row_base = local_x * (Z * D) + local_z + d * Z

    def shift_y(v, k):
        rolled = pltpu.roll(v, k % Y, 2)
        keep = lane >= k if k > 0 else lane < Y + k
        return jnp.where(keep, rolled, 0.0)

    def lateral(ref, out):
        def step(s, carry):
            x = s * R
            centre = ref[pl.ds(x + XP, R), ZI, :]
            total = (2.0 * second_coef[0]) * centre
            for k in range(1, 5):
                total = total + second_coef[k] * (
                    (ref[pl.ds(x + XP + k, R), ZI, :] + ref[pl.ds(x + XP - k, R), ZI, :])
                    + (shift_y(centre, k) + shift_y(centre, -k))
                )
            out[pl.ds(x, R)] = total
            return carry

        lax.fori_loop(0, S, step, 0)

    def vertical(ref, out, cross):
        def step(s, carry):
            x = s * R
            mid = pl.ds(x + XP, R)
            two = second_coef[0] * ref[mid, ZI, :]
            one = jnp.zeros_like(two)
            for k in range(1, 5):
                high = ref[mid, ZP + k : ZP + k + Z, :]
                low = ref[mid, ZP - k : ZP - k + Z, :]
                two = two + second_coef[k] * (high + low)
                one = one + first_coef[k - 1] * (high - low)
            out[pl.ds(x, R)] = two
            cross[mid] = one
            return carry

        lax.fori_loop(0, S, step, 0)

    def combine(s, lat, dz, cross):
        x = s * R
        here = pl.ds(x, R)
        total = jnp.zeros((R, Z, Y), jnp.float32)
        for k in range(1, 5):
            total = total + first_coef[k - 1] * (
                cross[pl.ds(x + XP + k, R)] - cross[pl.ds(x + XP - k, R)]
            )
        return coefs[1, here] * lat[here] + dz[here] + coefs[2, here] * total

    source_row = src_cell[0] // Y
    source_y = src_cell[0] - source_row * Y

    def source(s, n):
        hit = (row_base + s * (R * Z * D) == source_row) & (lane == source_y)
        return jnp.where(hit, src_wave[0, n], 0.0)

    lateral(eu0, lat_u)
    gather.forward_outer()
    lateral(ea0, lat_a)

    cells = rec_cell[...]
    rec_row = cells // Y
    rec_y = cells - rec_row * Y
    records = rec_data[0, 0:1, :]
    nrec = cells.shape[1]
    spread = (lax.broadcasted_iota(jnp.int32, (Y, nrec), 0) == rec_y).astype(jnp.float32)
    many = R * Z
    flat = lax.broadcasted_iota(jnp.int32, (many, nrec), 0)
    flat_row = (flat // Z) * (Z * D) + lax.rem(flat, Z) + d * Z

    def receivers(s, carry):
        plane = jnp.where(flat_row + s * (R * Z * D) == rec_row, records, 0.0)
        placed = lax.dot_general(
            plane, spread, (((1,), (1,)), ((), ())),
            precision=lax.Precision.HIGHEST, preferred_element_type=jnp.float32,
        )
        rec_field[pl.ds(s * R, R)] = placed.reshape(R, Z, Y)
        return carry

    lax.fori_loop(0, S, receivers, 0)
    gather.forward_inner()
    halo_u0.wait()
    vertical(eu0, dz_u, cr_u)
    halo_a0.wait()
    vertical(ea0, dz_a, cr_a)
    loads[6].wait()
    loads[7].wait()
    gather.finish()

    def first_u(s, carry):
        here, mid = pl.ds(s * R, R), pl.ds(s * R + XP, R)
        applied = combine(s, lat_u, dz_u, cr_u)
        grad[s // 2, lax.rem(s, 2)] = ea0[mid, ZI, :] * applied
        eu1[mid, ZI, :] = 2.0 * eu0[mid, ZI, :] - up[here] + coefs[0, here] * applied + source(s, 0)
        return carry

    lax.fori_loop(0, S, first_u, 0)
    halo_u1 = Halo(eu1, 4, 4, rows)
    halo_u1.start()
    gather_k.forward_outer()

    def first_a(s, carry):
        here, mid = pl.ds(s * R, R), pl.ds(s * R + XP, R)
        applied = combine(s, lat_a, dz_a, cr_a)
        a1[here] = 2.0 * ea0[mid, ZI, :] - ap[here] + coefs[0, here] * applied + rec_field[here]
        return carry

    lax.fori_loop(0, S, first_a, 0)
    lateral(eu1, lat_u)
    gather_k.forward_inner()
    halo_u1.wait()
    vertical(eu1, dz_u, cr_u)

    group = shot_group[0]
    weight = jnp.zeros((R, Z, Y), jnp.float32)
    for block in range(BK):
        level = jnp.float32(0.0)
        for b in range(NB):
            level = level + bins[group, block, b].astype(jnp.float32) * (2.0 ** (-b))
        weight = jnp.where(local_z // (Z // BK) == block, level, weight)

    def second_u(s, carry):
        here, mid = pl.ds(s * R, R), pl.ds(s * R + XP, R)
        applied = combine(s, lat_u, dz_u, cr_u)
        q, c = s // 2, lax.rem(s, 2)
        grad[q, c] = weight * (grad[q, c] + a1[here] * applied)
        eu2[mid, ZI, :] = (
            2.0 * eu1[mid, ZI, :] - eu0[mid, ZI, :] + coefs[0, here] * applied + source(s, 1)
        )
        return carry

    lax.fori_loop(0, S, second_u, 0)
    half = remote(
        grad.at[:, 1 - core], half_in, half_send, half_recv, (sid(outer, inner, 1 - core), d)
    )
    half.start()
    halo_u2 = Halo(eu2, 4, 6, rows)
    halo_u2.start()
    gather_k.finish()
    halo_k = Halo(eco, 1, 8, pl.ds(0, X))
    halo_k.start()

    half.wait_recv()

    def add_half(q, carry):
        part[q] = grad[q, core] + half_in[q]
        return carry

    lax.fori_loop(0, Q, add_half, 0)
    scatter = []
    for i in range(1, Q):
        target = lax.rem(chip + i, Q)
        copy = remote(
            part.at[target], block_in.at[i - 1], rs_send.at[i - 1], rs_recv.at[i - 1],
            (target * 2 + core, d),
        )
        copy.start()
        scatter.append(copy)

    lateral(eu2, lat_a)
    for copy in scatter:
        copy.wait_recv()
    total = part[chip]
    for i in range(1, Q):
        total = total + block_in[i - 1]
    es0[pl.ds(me * R + XP, R), ZI, :] = total
    gather_s = Gather(lambda s: es0.at[pl.ds(s * R + XP, R), ZI], s_send, s_recv)
    gather_s.start()
    halo_u2.wait()
    vertical(eu2, dz_u, cr_u)
    gather_s.forward_outer()

    def final_u(s, carry):
        here, mid = pl.ds(s * R, R), pl.ds(s * R + XP, R)
        lat_u[here] = coefs[0, here] * combine(s, lat_a, dz_u, cr_u)
        up[here] = 2.0 * eu2[mid, ZI, :] - eu1[mid, ZI, :] + source(s, 2)
        return carry

    lax.fori_loop(0, S, final_u, 0)
    gather_s.forward_inner()
    gather_s.finish()
    halo_s = Halo(es0, 2, 10, rows)
    halo_s.start()
    halo_k.wait()
    halo_s.wait()

    def relax(src, s, z0, count):
        mid = pl.ds(s * R + XP, R)
        centre = src[mid, z0 : z0 + count, :]
        ln = lax.broadcasted_iota(jnp.int32, centre.shape, 2)
        around = src[pl.ds(s * R + XP + 1, R), z0 : z0 + count, :]
        around = around + src[pl.ds(s * R + XP - 1, R), z0 : z0 + count, :]
        around = around + src[mid, z0 + 1 : z0 + 1 + count, :] + src[mid, z0 - 1 : z0 - 1 + count, :]
        around = around + jnp.where(ln >= 1, pltpu.roll(centre, 1, 2), 0.0)
        around = around + jnp.where(ln < Y - 1, pltpu.roll(centre, Y - 1, 2), 0.0)
        return centre + eco[pl.ds(s * R, R), z0 : z0 + count, :] * (around - 6.0 * centre)

    def sweep_one(s, carry):
        es1[pl.ds(s * R + XP, R), ZP - 4 : ZP + Z + 4, :] = relax(es0, s, ZP - 4, Z + 8)
        return carry

    lax.fori_loop(0, S, sweep_one, 0)

    def sweep_two(s, squares):
        smoothed = relax(es1, s, ZP, Z)
        lat_a[pl.ds(s * R, R)] = smoothed
        return squares + jnp.sum(smoothed * smoothed, axis=0)

    squares = lax.fori_loop(0, S, sweep_two, jnp.zeros((Z, Y), jnp.float32))
    sq[0] = squares
    sums = []
    for i in range(1, D):
        copy = remote(
            sq.at[0], sq.at[i], sq_send.at[i - 1], sq_recv.at[i - 1], (me, lax.rem(d + i, D))
        )
        copy.start()
        sums.append(copy)
    for copy in sums:
        copy.wait_recv()
    for i in range(1, D):
        squares = squares + sq[i]
    mean = jnp.sum(squares) * (1.0 / (X * Z * D * Y))
    inverse = lax.rsqrt(jnp.full((R, Z, Y), mean + 1e-06, jnp.float32))

    def final(s, carry):
        here = pl.ds(s * R, R)
        wave = up[here] + lat_u[here] * (1.0 - 0.25 * jnp.tanh(lat_a[here] * inverse))
        dz_a[here] = wave
        return carry

    lax.fori_loop(0, S, final, 0)
    direction = lat_a[own] * inverse
    grad_own[...] = direction
    model_own[...] = coefs[0, own] * (1.0 - 0.25 * jnp.tanh(direction))
    outs = [
        pltpu.make_async_copy(dz_a, wave_next.at[0], out_sem.at[0]),
        pltpu.make_async_copy(model_own, model_next, out_sem.at[1]),
        pltpu.make_async_copy(grad_own, grad_dir, out_sem.at[2]),
    ]
    for copy in outs:
        copy.start()
    for one in (gather, gather_k, gather_s, halo_u0, halo_a0, halo_u1, halo_u2, halo_k, halo_s):
        one.drain()
    half.wait_send()
    for copy in scatter + sums:
        copy.wait_send()
    for copy in outs:
        copy.wait()


def solution(mesh):
    S, D = mesh.shape["shot"], mesh.shape["depth"]
    Q, O = S // 2, S // 4

    def body(u_prev, u_cur, a_prev, a_cur, model, *rest):
        _, X, Z, Y = u_cur.shape
        R = model.shape[0]
        bins = rest[3]
        dims = (S, D, R, X, Z, Y, bins.shape[2], bins.shape[1])
        f32 = jnp.float32
        field = pltpu.VMEM((X, Z, Y), f32)
        extended = pltpu.VMEM((X + 2 * XP, Z + 2 * ZP, Y), f32)
        crossing = pltpu.VMEM((X + 2 * XP, Z, Y), f32)
        dma = pltpu.SemaphoreType.DMA
        hbm = pl.BlockSpec(memory_space=pl.ANY)
        smem = pl.BlockSpec(memory_space=pltpu.SMEM)
        vmem = pl.BlockSpec(memory_space=pltpu.VMEM)
        return pl.pallas_call(
            functools.partial(kernel, dims),
            out_shape=(
                jax.ShapeDtypeStruct(model.shape, f32),
                jax.ShapeDtypeStruct(model.shape, f32),
                jax.ShapeDtypeStruct(u_cur.shape, f32),
            ),
            in_specs=[hbm] * 8 + [smem, smem, smem, vmem, smem, vmem],
            out_specs=[hbm] * 3,
            scratch_shapes=[
                extended,
                extended,
                extended,
                extended,
                field,
                field,
                pltpu.VMEM((3, X, Z, Y), f32),
                pltpu.VMEM((X, Z + 2 * ZP, Y), f32),
                field,
                field,
                crossing,
                field,
                field,
                crossing,
                field,
                field,
                pltpu.VMEM((Q, 2, R, Z, Y), f32),
                pltpu.VMEM((Q, R, Z, Y), f32),
                pltpu.VMEM((Q, R, Z, Y), f32),
                pltpu.VMEM((Q - 1, R, Z, Y), f32),
                extended,
                extended,
                pltpu.VMEM((D, Z, Y), f32),
                pltpu.VMEM((R, Z, Y), f32),
                pltpu.VMEM((R, Z, Y), f32),
                dma((8,)),
                dma((12,)),
                dma((12,)),
                dma((4 * O,)),
                dma((4 * O,)),
                dma((4 * O,)),
                dma((4 * O,)),
                dma((4 * O,)),
                dma((4 * O,)),
                dma,
                dma,
                dma((Q - 1,)),
                dma((Q - 1,)),
                dma((D - 1,)),
                dma((D - 1,)),
                dma((3,)),
            ],
            compiler_params=pltpu.CompilerParams(
                collective_id=0, has_side_effects=True, vmem_limit_bytes=40 * 1024 * 1024
            ),
        )(u_prev, u_cur, a_prev, a_cur, model, *rest)

    return jax.shard_map(
        body,
        mesh=mesh,
        in_specs=(P("shot", None, "depth", None),) * 4
        + (P("shot", "depth", None),) * 4
        + (
            P(None, "depth", None),
            P("shot"),
            P("shot"),
            P("shot", None),
            P("shot", None),
            P("shot", None, None),
        ),
        out_specs=(
            P("shot", "depth", None),
            P("shot", "depth", None),
            P("shot", None, "depth", None),
        ),
        check_vma=False,
    )
```

time: 269 us -> 74.5 us (0.28)
  blocking collectives: 89.2 us -> 0 us
  waiting for transfers between devices: 88.7 us -> 0 us
  Pallas kernels: 0 us -> 61.9 us
  other arithmetic: 39.6 us -> 0 us
  starting transfers between devices: 25.9 us -> 0 us
  between operations: 16.5 us -> 1.98 us
  local copies, waits for them, and re-layouts: 6.2 us -> 10 us
    psum x1 -> x0, waiting for transfers between devices: 85.6 us -> none  [body(): smoothed = lax.psum(local_sum, 'shot')]
    all_gather x4 -> x0, blocking collectives: 83.7 us -> none  [the longest x1 24.4 us: body(): lax.all_gather(model, 'shot', axis=0, tiled=True)]
    pallas_call x0 -> x1, Pallas kernels: none -> 61.9 us  [body(): pl.pallas_call(functools.partial(kernel, dims), out_shape=(jax.ShapeDtype...]
    add x8 -> x0, other arithmetic: 28.1 us -> none  [the longest x1 12.4 us: body(): 2.0 * wave_pair[0] - old_pair[0] + model_full * final_applied]
    ppermute x10 -> x0, starting transfers between devices: 25.9 us -> none  [the longest x5 19.4 us: extended(): lax.ppermute(lax.slice_in_dim(block, block.shape[dim] - width, None, axis...]
    unnamed x38 -> x26, local copies, waits for them, and re-layouts: 1.65 us -> 10 us
    psum x1 -> x0, blocking collectives: 5.55 us -> none  [body(): square_sum = lax.psum(jnp.sum(smoothed * smoothed), 'depth')]
    slice x5 -> x0, local copies, waits for them, and re-layouts: 3.75 us -> none  [the longest x4 3.17 us: extended(): lax.slice_in_dim(block, block.shape[dim] - width, None, axis=dim)]
  transfers between devices with their start and end apart: 11 -> 0, of which waited for: 2 -> 0; matrix products, arithmetic and copies ran while one was open for 5% -> 0% of each run, Pallas kernels for 0% -> 0%
where the time goes in v1:
time: 74.5 us; the launch traced here: 73.9 us
  Pallas kernels  61.9 us (83%)
  local copies, waits for them, and re-layouts  10 us (13%)
  between operations  1.98 us (3%)
    pallas_call x1, Pallas kernels, body(): pl.pallas_call(functools.partial(kernel, dims), out_shape=(jax.ShapeDtype...  61.9 us
    unnamed x26, local copies, waits for them, and re-layouts  10 us

profile of v1, /device:TPU:0, one launch (start us, length us, event | category | flops | bytes accessed | tf_op | source)
XLA Modules:
  0.0 73.9 jit_solution(4348840916658190224)
XLA Ops:
  1.9 0.0 copy-start.8
  1.9 0.0 copy-start.9
  1.9 0.0 copy-start.10
  2.0 0.8 %copy.17.bins = s32[16,2,4]{2,1,0:T(2,128)S(1)} copy(s32[16,2,4]{0,2,1:T(4,128)} %param.22) | data formatting | bytes 1024 | tf_op args[8]
  2.7 0.0 copy-done.8
  2.7 0.0 copy-done.9
  2.8 0.0 copy-done.10
  2.8 0.0 copy-start
  2.8 1.0 %copy-done = f32[1,64,16,128]{3,2,1,0:T(8,128)S(1)} copy-done((f32[1,64,16,128]{3,2,1,0:T(8,128)S(1)}, f32[1,64,16,128]{3,2,1,0:T(8,128)}, u32[]{:S(2)}) %copy-start) | copy-done | bytes 524312
  3.8 0.0 copy-start.1
  3.8 1.0 %copy-done.1 = f32[1,64,16,128]{3,2,1,0:T(8,128)S(1)} copy-done((f32[1,64,16,128]{3,2,1,0:T(8,128)S(1)}, f32[1,64,16,128]{3,2,1,0:T(8,128)}, u32[]{:S(2)}) %copy-start.1) | copy-done | bytes 524312
  4.8 0.0 copy-start.2
  4.8 1.0 %copy-done.2 = f32[1,64,16,128]{3,2,1,0:T(8,128)S(1)} copy-done((f32[1,64,16,128]{3,2,1,0:T(8,128)S(1)}, f32[1,64,16,128]{3,2,1,0:T(8,128)}, u32[]{:S(2)}) %copy-start.2) | copy-done | bytes 524312
  5.9 0.0 copy-start.3
  5.9 1.0 %copy-done.3 = f32[1,64,16,128]{3,2,1,0:T(8,128)S(1)} copy-done((f32[1,64,16,128]{3,2,1,0:T(8,128)S(1)}, f32[1,64,16,128]{3,2,1,0:T(8,128)}, u32[]{:S(2)}) %copy-start.3) | copy-done | bytes 524312
  6.9 0.0 copy-start.4
  6.9 0.8 %copy-done.4 = f32[4,16,128]{2,1,0:T(8,128)S(1)} copy-done((f32[4,16,128]{2,1,0:T(8,128)S(1)}, f32[4,16,128]{2,1,0:T(8,128)}, u32[]{:S(2)}) %copy-start.4) | copy-done | bytes 32792
  7.7 0.0 copy-start.5
  7.7 0.8 %copy-done.5 = f32[4,16,128]{2,1,0:T(8,128)S(1)} copy-done((f32[4,16,128]{2,1,0:T(8,128)S(1)}, f32[4,16,128]{2,1,0:T(8,128)}, u32[]{:S(2)}) %copy-start.5) | copy-done | bytes 32792
  8.4 0.0 copy-start.6
  8.4 0.8 %copy-done.6 = f32[4,16,128]{2,1,0:T(8,128)S(1)} copy-done((f32[4,16,128]{2,1,0:T(8,128)S(1)}, f32[4,16,128]{2,1,0:T(8,128)}, u32[]{:S(2)}) %copy-start.6) | copy-done | bytes 32792
  9.2 0.0 copy-start.7
  9.2 0.8 %copy-done.7 = f32[4,16,128]{2,1,0:T(8,128)S(1)} copy-done((f32[4,16,128]{2,1,0:T(8,128)S(1)}, f32[4,16,128]{2,1,0:T(8,128)}, u32[]{:S(2)}) %copy-start.7) | copy-done | bytes 32792
  10.0 61.9 %shard_map.157 = (f32[4,16,128]{2,1,0:T(8,128)S(1)}, f32[4,16,128]{2,1,0:T(8,128)S(1)}, f32[1,64,16,128]{3,2,1,0:T(8,128)S(1)}) custom-call(f32[1,64,16,128]{3,2,1,0:T(8,128)S(1)} %copy-done, f32[1,64,16,128]{3,2,1,0:T(8,128)S(1)} %copy-done.1, f32[1,64,16,128]{3,2,1,0:T(8,128)S(1)} %copy-done.2, f32[1,64,16,128]{3,2,1,0:T(8,128)S(1)} %copy-done.3, ...), custom_call_target="tpu_custom_call" | custom-call | tf_op jit(solution)/shard_map/pallas_call | solution.py:493
  71.8 0.6 copy.23
  72.5 0.6 copy.24
  73.1 0.8 %copy.25 = f32[1,64,16,128]{3,2,1,0:T(8,128)} copy(f32[1,64,16,128]{3,2,1,0:T(8,128)S(1)} %get-tuple-element.8) | data formatting | bytes 1048576
Async XLA Ops:
  1.9 0.8 %copy-start.8 = (f32[1,2,128]{2,1,0:T(2,128)S(1)}, f32[1,2,128]{2,1,0:T(2,128)}, u32[]{:S(2)}) copy-start(f32[1,2,128]{2,1,0:T(2,128)} %rec_data.1) | copy-start | bytes 3076
  1.9 0.8 %copy-start.9 = (s32[1,128]{1,0:T(1,128)S(1)}, s32[1,128]{1,0:T(1,128)}, u32[]{:S(2)}) copy-start(s32[1,128]{1,0:T(1,128)} %rec_cell.1) | copy-start | bytes 1540
  1.9 0.8 %copy-start.10 = (f32[1,3]{1,0:T(1,128)S(1)}, f32[1,3]{1,0:T(1,128)}, u32[]{:S(2)}) copy-start(f32[1,3]{1,0:T(1,128)} %src_wave.1) | copy-start | bytes 40
  2.8 1.0 %copy-start = (f32[1,64,16,128]{3,2,1,0:T(8,128)S(1)}, f32[1,64,16,128]{3,2,1,0:T(8,128)}, u32[]{:S(2)}) copy-start(f32[1,64,16,128]{3,2,1,0:T(8,128)} %u_prev.1) | copy-start | bytes 1572868
  3.8 1.0 %copy-start.1 = (f32[1,64,16,128]{3,2,1,0:T(8,128)S(1)}, f32[1,64,16,128]{3,2,1,0:T(8,128)}, u32[]{:S(2)}) copy-start(f32[1,64,16,128]{3,2,1,0:T(8,128)} %u_cur.1) | copy-start | bytes 1572868
  4.8 1.0 %copy-start.2 = (f32[1,64,16,128]{3,2,1,0:T(8,128)S(1)}, f32[1,64,16,128]{3,2,1,0:T(8,128)}, u32[]{:S(2)}) copy-start(f32[1,64,16,128]{3,2,1,0:T(8,128)} %a_prev.1) | copy-start | bytes 1572868
  5.9 1.0 %copy-start.3 = (f32[1,64,16,128]{3,2,1,0:T(8,128)S(1)}, f32[1,64,16,128]{3,2,1,0:T(8,128)}, u32[]{:S(2)}) copy-start(f32[1,64,16,128]{3,2,1,0:T(8,128)} %a_cur.1) | copy-start | bytes 1572868
  6.9 0.8 %copy-start.4 = (f32[4,16,128]{2,1,0:T(8,128)S(1)}, f32[4,16,128]{2,1,0:T(8,128)}, u32[]{:S(2)}) copy-start(f32[4,16,128]{2,1,0:T(8,128)} %model.1) | copy-start | bytes 98308
  7.7 0.8 %copy-start.5 = (f32[4,16,128]{2,1,0:T(8,128)S(1)}, f32[4,16,128]{2,1,0:T(8,128)}, u32[]{:S(2)}) copy-start(f32[4,16,128]{2,1,0:T(8,128)} %aniso_h.1) | copy-start | bytes 98308
  8.4 0.8 %copy-start.6 = (f32[4,16,128]{2,1,0:T(8,128)S(1)}, f32[4,16,128]{2,1,0:T(8,128)}, u32[]{:S(2)}) copy-start(f32[4,16,128]{2,1,0:T(8,128)} %aniso_c.1) | copy-start | bytes 98308
  9.2 0.8 %copy-start.7 = (f32[4,16,128]{2,1,0:T(8,128)S(1)}, f32[4,16,128]{2,1,0:T(8,128)}, u32[]{:S(2)}) copy-start(f32[4,16,128]{2,1,0:T(8,128)} %smooth_coef.1) | copy-start | bytes 98308

commit v2 on v1

--- a/solution.py
+++ b/solution.py
@@ -40,7 +40,8 @@
     up,
     ap,
     coefs,
-    eco,
+    ec,
+    band,
     lat_u,
     dz_u,
     cr_u,
@@ -53,27 +54,28 @@
     half_in,
     part,
     block_in,
-    es0,
-    es1,
-    sq,
-    model_own,
-    grad_own,
+    eb,
+    eb1,
+    smooth,
+    sqd,
+    sqs,
     load_sem,
     halo_send,
     halo_recv,
     g_send,
     g_recv,
-    k_send,
-    k_recv,
+    rim_send,
+    rim_recv,
     s_send,
     s_recv,
     half_send,
     half_recv,
     rs_send,
     rs_recv,
-    sq_send,
-    sq_recv,
-    out_sem,
+    sqd_send,
+    sqd_recv,
+    sqs_send,
+    sqs_recv,
 ):
     S, D, R, X, Z, Y, NB, BK = dims
     Q = S // 2
@@ -94,7 +96,7 @@
         pltpu.make_async_copy(model, coefs.at[0, own], load_sem.at[0]),
         pltpu.make_async_copy(aniso_h, coefs.at[1, own], load_sem.at[1]),
         pltpu.make_async_copy(aniso_c, coefs.at[2, own], load_sem.at[2]),
-        pltpu.make_async_copy(smooth_coef, eco.at[own, ZI], load_sem.at[3]),
+        pltpu.make_async_copy(smooth_coef, ec.at[pl.ds(2, R), ZI], load_sem.at[3]),
         pltpu.make_async_copy(u_cur.at[0], eu0.at[pl.ds(XP, X), ZI], load_sem.at[4]),
         pltpu.make_async_copy(a_cur.at[0], ea0.at[pl.ds(XP, X), ZI], load_sem.at[5]),
         pltpu.make_async_copy(u_prev.at[0], up, load_sem.at[6]),
@@ -104,20 +106,22 @@
         load.start()
 
     def zero_z(i, carry):
-        for ref in (eu0, eu1, eu2, ea0, es0, es1):
+        for ref in (eu0, eu1, eu2, ea0):
             ref[i, 0:ZP, :] = jnp.zeros((ZP, Y), jnp.float32)
             ref[i, ZP + Z :, :] = jnp.zeros((ZP, Y), jnp.float32)
         return carry
 
     lax.fori_loop(0, X + 2 * XP, zero_z, 0)
 
-    def zero_c(i, carry):
-        eco[i, 0:ZP, :] = jnp.zeros((ZP, Y), jnp.float32)
-        eco[i, ZP + Z :, :] = jnp.zeros((ZP, Y), jnp.float32)
-        return carry
-
-    lax.fori_loop(0, X, zero_c, 0)
-    for ref in (eu0, eu1, eu2, ea0, es0, es1):
+    tall = jnp.zeros((2, Z + 2 * ZP, Y), jnp.float32)
+    side = jnp.zeros((R, ZP, Y), jnp.float32)
+    for ref in (eb, ec):
+        ref[0:2] = tall
+        ref[R + 2 : R + 4] = tall
+        ref[2 : R + 2, 0:ZP, :] = side
+        ref[2 : R + 2, ZP + Z :, :] = side
+
+    for ref in (eu0, eu1, eu2, ea0):
         for i in list(range(XP)) + list(range(XP + X, X + 2 * XP)):
             ref[i, ZI, :] = jnp.zeros((Z, Y), jnp.float32)
     for ref in (cr_u, cr_a):
@@ -125,11 +129,11 @@
             ref[i] = jnp.zeros((Z, Y), jnp.float32)
 
     barrier = pltpu.get_barrier_semaphore()
-    peers = [(sid(outer, inner, 1 - core), d)]
-    for i in range(1, Q):
-        peers.append((lax.rem(chip + i, Q) * 2 + core, d))
-    for i in range(1, D):
-        peers.append((me, lax.rem(d + i, D)))
+    peers = [(lax.rem(me + i, S), d) for i in range(1, S)]
+    peers += [(me, lax.rem(d + i, D)) for i in range(1, D)]
+    for dz in sorted({1, D - 1}):
+        for dx in (1, S - 1):
+            peers.append((lax.rem(me + dx, S), lax.rem(d + dz, D)))
     for peer in peers:
         pl.semaphore_signal(barrier, inc=1, device_id=peer, device_id_type=MESH)
     pl.semaphore_wait(barrier, len(peers))
@@ -154,7 +158,7 @@
             remote(ref, ref, self.send.at[sem], self.recv.at[sem], (me, d)).wait_recv()
 
         def start(self):
-            for i in range(1, O):
+            for i in sorted(range(1, O), key=lambda i: min(i, O - i)):
                 self.go(me, i, (sid(lax.rem(outer + i, O), inner, core), d))
             self.go(me, O, (sid(outer, 1 - inner, core), d))
             self.go(me, 2 * O, (sid(outer, inner, 1 - core), d))
@@ -204,6 +208,41 @@
         def drain(self):
             pl.when(d < D - 1)(lambda: self.up.wait_send())
             pl.when(d > 0)(lambda: self.down.wait_send())
+
+    class Rim:
+        def __init__(self, ref, slot):
+            self.parts = []
+            for dx in (-1, 0, 1):
+                for dz in (-1, 0, 1):
+                    if dx == 0 and dz == 0:
+                        continue
+                    n = slot + len(self.parts)
+                    xs, xd = {-1: ((2, 2), (R + 2, 2)), 0: ((2, R), (2, R)), 1: ((R, 2), (0, 2))}[dx]
+                    zs, zd = {
+                        -1: ((ZP, 2), (ZP + Z, 2)), 0: ((ZP, Z), (ZP, Z)), 1: ((ZP + Z - 2, 2), (ZP - 2, 2))
+                    }[dz]
+                    ts, td = me + dx, d + dz
+                    goes = (ts >= 0) & (ts < S) & (td >= 0) & (td < D)
+                    fs, fd = me - dx, d - dz
+                    comes = (fs >= 0) & (fs < S) & (fd >= 0) & (fd < D)
+                    copy = remote(
+                        ref.at[pl.ds(*xs), pl.ds(*zs)], ref.at[pl.ds(*xd), pl.ds(*zd)],
+                        rim_send.at[n], rim_recv.at[n],
+                        (jnp.clip(ts, 0, S - 1), jnp.clip(td, 0, D - 1)),
+                    )
+                    self.parts.append((copy, goes, comes))
+
+        def start(self):
+            for copy, goes, comes in self.parts:
+                pl.when(goes)(copy.start)
+
+        def wait(self):
+            for copy, goes, comes in self.parts:
+                pl.when(comes)(copy.wait_recv)
+
+        def drain(self):
+            for copy, goes, comes in self.parts:
+                pl.when(goes)(copy.wait_send)
 
     rows = pl.ds(XP, X)
     for load in loads[:3]:
@@ -217,33 +256,47 @@
     halo_a0 = Halo(ea0, 4, 2, rows)
     halo_a0.start()
     loads[3].wait()
-    gather_k = Gather(lambda s: eco.at[pl.ds(s * R, R), ZI], k_send, k_recv)
-    gather_k.start()
+    rim_k = Rim(ec, 0)
+    rim_k.start()
 
     lane = lax.broadcasted_iota(jnp.int32, (R, Z, Y), 2)
     local_x = lax.broadcasted_iota(jnp.int32, (R, Z, Y), 0)
     local_z = lax.broadcasted_iota(jnp.int32, (R, Z, Y), 1)
     row_base = local_x * (Z * D) + local_z + d * Z
 
-    def shift_y(v, k):
-        rolled = pltpu.roll(v, k % Y, 2)
-        keep = lane >= k if k > 0 else lane < Y + k
-        return jnp.where(keep, rolled, 0.0)
+    gap = lax.abs(
+        lax.broadcasted_iota(jnp.int32, (Y, Y), 0) - lax.broadcasted_iota(jnp.int32, (Y, Y), 1)
+    )
+    exact = jnp.where(gap == 0, 2.0 * second_coef[0], 0.0)
+    for k in range(1, 5):
+        exact = jnp.where(gap == k, second_coef[k], exact)
+    head = exact.astype(jnp.bfloat16)
+    rest = (exact - head.astype(jnp.float32)).astype(jnp.bfloat16)
+    band[0:Y, 0:Y] = head
+    band[Y:, 0:Y] = head
+    band[0:Y, Y:] = rest
+    band[Y:, Y:] = jnp.zeros((Y, Y), jnp.bfloat16)
+
+    def halves(v):
+        top = v.astype(jnp.bfloat16)
+        return jnp.concatenate([top, (v - top.astype(jnp.float32)).astype(jnp.bfloat16)], axis=-1)
+
+    CH = 16 if X % 16 == 0 else R
 
     def lateral(ref, out):
-        def step(s, carry):
-            x = s * R
-            centre = ref[pl.ds(x + XP, R), ZI, :]
-            total = (2.0 * second_coef[0]) * centre
+        def step(i, carry):
+            x = i * CH
+            centre = ref[pl.ds(x + XP, CH), ZI, :].reshape(CH * Z, Y)
+            both = jnp.dot(halves(centre), band[...], preferred_element_type=jnp.float32)
+            total = (both[:, :Y] + both[:, Y:]).reshape(CH, Z, Y)
             for k in range(1, 5):
                 total = total + second_coef[k] * (
-                    (ref[pl.ds(x + XP + k, R), ZI, :] + ref[pl.ds(x + XP - k, R), ZI, :])
-                    + (shift_y(centre, k) + shift_y(centre, -k))
+                    ref[pl.ds(x + XP + k, CH), ZI, :] + ref[pl.ds(x + XP - k, CH), ZI, :]
                 )
-            out[pl.ds(x, R)] = total
+            out[pl.ds(x, CH)] = total
             return carry
 
-        lax.fori_loop(0, S, step, 0)
+        lax.fori_loop(0, X // CH, step, 0)
 
     def vertical(ref, out, cross):
         def step(s, carry):
@@ -289,20 +342,22 @@
     records = rec_data[0, 0:1, :]
     nrec = cells.shape[1]
     spread = (lax.broadcasted_iota(jnp.int32, (Y, nrec), 0) == rec_y).astype(jnp.float32)
-    many = R * Z
+    spread = spread.astype(jnp.bfloat16)
+    spread = jnp.concatenate([spread, spread], axis=1)
+    many = CH * Z
     flat = lax.broadcasted_iota(jnp.int32, (many, nrec), 0)
     flat_row = (flat // Z) * (Z * D) + lax.rem(flat, Z) + d * Z
 
     def receivers(s, carry):
-        plane = jnp.where(flat_row + s * (R * Z * D) == rec_row, records, 0.0)
+        plane = halves(jnp.where(flat_row + s * (CH * Z * D) == rec_row, records, 0.0))
         placed = lax.dot_general(
             plane, spread, (((1,), (1,)), ((), ())),
-            precision=lax.Precision.HIGHEST, preferred_element_type=jnp.float32,
+            preferred_element_type=jnp.float32,
         )
-        rec_field[pl.ds(s * R, R)] = placed.reshape(R, Z, Y)
-        return carry
-
-    lax.fori_loop(0, S, receivers, 0)
+        rec_field[pl.ds(s * CH, CH)] = placed.reshape(CH, Z, Y)
+        return carry
+
+    lax.fori_loop(0, X // CH, receivers, 0)
     gather.forward_inner()
     halo_u0.wait()
     vertical(eu0, dz_u, cr_u)
@@ -322,7 +377,6 @@
     lax.fori_loop(0, S, first_u, 0)
     halo_u1 = Halo(eu1, 4, 4, rows)
     halo_u1.start()
-    gather_k.forward_outer()
 
     def first_a(s, carry):
         here, mid = pl.ds(s * R, R), pl.ds(s * R + XP, R)
@@ -332,17 +386,19 @@
 
     lax.fori_loop(0, S, first_a, 0)
     lateral(eu1, lat_u)
-    gather_k.forward_inner()
     halo_u1.wait()
     vertical(eu1, dz_u, cr_u)
 
     group = shot_group[0]
+    marks = bins[group].astype(jnp.float32)
+    power = lax.broadcasted_iota(jnp.int32, (BK, NB), 1)
+    scale = jnp.zeros((BK, NB), jnp.float32)
+    for b in range(NB):
+        scale = jnp.where(power == b, 2.0 ** (-b), scale)
+    levels = jnp.sum(marks * scale, axis=1, keepdims=True)
     weight = jnp.zeros((R, Z, Y), jnp.float32)
     for block in range(BK):
-        level = jnp.float32(0.0)
-        for b in range(NB):
-            level = level + bins[group, block, b].astype(jnp.float32) * (2.0 ** (-b))
-        weight = jnp.where(local_z // (Z // BK) == block, level, weight)
+        weight = jnp.where(local_z // (Z // BK) == block, levels[block : block + 1, 0:1], weight)
 
     def second_u(s, carry):
         here, mid = pl.ds(s * R, R), pl.ds(s * R + XP, R)
@@ -361,9 +417,6 @@
     half.start()
     halo_u2 = Halo(eu2, 4, 6, rows)
     halo_u2.start()
-    gather_k.finish()
-    halo_k = Halo(eco, 1, 8, pl.ds(0, X))
-    halo_k.start()
 
     half.wait_recv()
 
@@ -388,89 +441,83 @@
     total = part[chip]
     for i in range(1, Q):
         total = total + block_in[i - 1]
-    es0[pl.ds(me * R + XP, R), ZI, :] = total
-    gather_s = Gather(lambda s: es0.at[pl.ds(s * R + XP, R), ZI], s_send, s_recv)
-    gather_s.start()
+    eb[2 : R + 2, ZI, :] = total
+    rim_s = Rim(eb, 8)
+    rim_s.start()
+    rim_k.wait()
     halo_u2.wait()
     vertical(eu2, dz_u, cr_u)
-    gather_s.forward_outer()
-
-    def final_u(s, carry):
-        here, mid = pl.ds(s * R, R), pl.ds(s * R + XP, R)
-        lat_u[here] = coefs[0, here] * combine(s, lat_a, dz_u, cr_u)
-        up[here] = 2.0 * eu2[mid, ZI, :] - eu1[mid, ZI, :] + source(s, 2)
-        return carry
-
-    lax.fori_loop(0, S, final_u, 0)
-    gather_s.forward_inner()
-    gather_s.finish()
-    halo_s = Halo(es0, 2, 10, rows)
-    halo_s.start()
-    halo_k.wait()
-    halo_s.wait()
-
-    def relax(src, s, z0, count):
-        mid = pl.ds(s * R + XP, R)
-        centre = src[mid, z0 : z0 + count, :]
+    rim_s.wait()
+
+    def relax(src, x0, nx, z0, count):
+        centre = src[x0 : x0 + nx, z0 : z0 + count, :]
         ln = lax.broadcasted_iota(jnp.int32, centre.shape, 2)
-        around = src[pl.ds(s * R + XP + 1, R), z0 : z0 + count, :]
-        around = around + src[pl.ds(s * R + XP - 1, R), z0 : z0 + count, :]
-        around = around + src[mid, z0 + 1 : z0 + 1 + count, :] + src[mid, z0 - 1 : z0 - 1 + count, :]
+        around = src[x0 + 1 : x0 + 1 + nx, z0 : z0 + count, :]
+        around = around + src[x0 - 1 : x0 - 1 + nx, z0 : z0 + count, :]
+        around = around + src[x0 : x0 + nx, z0 + 1 : z0 + 1 + count, :]
+        around = around + src[x0 : x0 + nx, z0 - 1 : z0 - 1 + count, :]
         around = around + jnp.where(ln >= 1, pltpu.roll(centre, 1, 2), 0.0)
         around = around + jnp.where(ln < Y - 1, pltpu.roll(centre, Y - 1, 2), 0.0)
-        return centre + eco[pl.ds(s * R, R), z0 : z0 + count, :] * (around - 6.0 * centre)
-
-    def sweep_one(s, carry):
-        es1[pl.ds(s * R + XP, R), ZP - 4 : ZP + Z + 4, :] = relax(es0, s, ZP - 4, Z + 8)
-        return carry
-
-    lax.fori_loop(0, S, sweep_one, 0)
-
-    def sweep_two(s, squares):
-        smoothed = relax(es1, s, ZP, Z)
-        lat_a[pl.ds(s * R, R)] = smoothed
-        return squares + jnp.sum(smoothed * smoothed, axis=0)
-
-    squares = lax.fori_loop(0, S, sweep_two, jnp.zeros((Z, Y), jnp.float32))
-    sq[0] = squares
+        return centre + ec[x0 : x0 + nx, z0 : z0 + count, :] * (around - 6.0 * centre)
+
+    eb1[1 : R + 3, ZP - 4 : ZP + Z + 4, :] = relax(eb, 1, R + 2, ZP - 4, Z + 8)
+    smoothed = relax(eb1, 2, R, ZP, Z)
+    smooth[own] = smoothed
+    gather_s = Gather(lambda s: smooth.at[pl.ds(s * R, R)], s_send, s_recv)
+    gather_s.start()
+    squares = jnp.sum((smoothed * smoothed).reshape(R * Z // 8, 8, Y), axis=0)
+    sqd[0] = squares
     sums = []
     for i in range(1, D):
         copy = remote(
-            sq.at[0], sq.at[i], sq_send.at[i - 1], sq_recv.at[i - 1], (me, lax.rem(d + i, D))
+            sqd.at[0], sqd.at[i], sqd_send.at[i - 1], sqd_recv.at[i - 1], (me, lax.rem(d + i, D))
         )
         copy.start()
         sums.append(copy)
     for copy in sums:
         copy.wait_recv()
     for i in range(1, D):
-        squares = squares + sq[i]
+        squares = squares + sqd[i]
+    sqs[0] = squares
+    slab = []
+    for i in range(1, S):
+        copy = remote(
+            sqs.at[0], sqs.at[i], sqs_send.at[i - 1], sqs_recv.at[i - 1], (lax.rem(me + i, S), d)
+        )
+        copy.start()
+        slab.append(copy)
+    gather_s.forward_outer()
+
+    def final_u(s, carry):
+        here, mid = pl.ds(s * R, R), pl.ds(s * R + XP, R)
+        lat_u[here] = coefs[0, here] * combine(s, lat_a, dz_u, cr_u)
+        up[here] = 2.0 * eu2[mid, ZI, :] - eu1[mid, ZI, :] + source(s, 2)
+        return carry
+
+    lax.fori_loop(0, S, final_u, 0)
+    gather_s.forward_inner()
+    for copy in slab:
+        copy.wait_recv()
+    for i in range(1, S):
+        squares = squares + sqs[i]
     mean = jnp.sum(squares) * (1.0 / (X * Z * D * Y))
     inverse = lax.rsqrt(jnp.full((R, Z, Y), mean + 1e-06, jnp.float32))
+    direction = smoothed * inverse
+    grad_dir[...] = direction
+    model_next[...] = coefs[0, own] * (1.0 - 0.25 * jnp.tanh(direction))
+    gather_s.finish()
 
     def final(s, carry):
         here = pl.ds(s * R, R)
-        wave = up[here] + lat_u[here] * (1.0 - 0.25 * jnp.tanh(lat_a[here] * inverse))
-        dz_a[here] = wave
+        wave_next[0, here] = up[here] + lat_u[here] * (1.0 - 0.25 * jnp.tanh(smooth[here] * inverse))
         return carry
 
     lax.fori_loop(0, S, final, 0)
-    direction = lat_a[own] * inverse
-    grad_own[...] = direction
-    model_own[...] = coefs[0, own] * (1.0 - 0.25 * jnp.tanh(direction))
-    outs = [
-        pltpu.make_async_copy(dz_a, wave_next.at[0], out_sem.at[0]),
-        pltpu.make_async_copy(model_own, model_next, out_sem.at[1]),
-        pltpu.make_async_copy(grad_own, grad_dir, out_sem.at[2]),
-    ]
-    for copy in outs:
-        copy.start()
-    for one in (gather, gather_k, gather_s, halo_u0, halo_a0, halo_u1, halo_u2, halo_k, halo_s):
+    for one in (gather, gather_s, halo_u0, halo_a0, halo_u1, halo_u2, rim_k, rim_s):
         one.drain()
     half.wait_send()
-    for copy in scatter + sums:
+    for copy in scatter + sums + slab:
         copy.wait_send()
-    for copy in outs:
-        copy.wait()
 
 
 def solution(mesh):
@@ -487,7 +534,7 @@
         extended = pltpu.VMEM((X + 2 * XP, Z + 2 * ZP, Y), f32)
         crossing = pltpu.VMEM((X + 2 * XP, Z, Y), f32)
         dma = pltpu.SemaphoreType.DMA
-        hbm = pl.BlockSpec(memory_space=pl.ANY)
+        hbm = pl.BlockSpec(memory_space=pltpu.HBM)
         smem = pl.BlockSpec(memory_space=pltpu.SMEM)
         vmem = pl.BlockSpec(memory_space=pltpu.VMEM)
         return pl.pallas_call(
@@ -497,8 +544,8 @@
                 jax.ShapeDtypeStruct(model.shape, f32),
                 jax.ShapeDtypeStruct(u_cur.shape, f32),
             ),
-            in_specs=[hbm] * 8 + [smem, smem, smem, vmem, smem, vmem],
-            out_specs=[hbm] * 3,
+            in_specs=[hbm] * 8 + [vmem, smem, smem, vmem, smem, vmem],
+            out_specs=[vmem] * 3,
             scratch_shapes=[
                 extended,
                 extended,
@@ -507,7 +554,8 @@
                 field,
                 field,
                 pltpu.VMEM((3, X, Z, Y), f32),
-                pltpu.VMEM((X, Z + 2 * ZP, Y), f32),
+                pltpu.VMEM((R + 4, Z + 2 * ZP, Y), f32),
+                pltpu.VMEM((2 * Y, 2 * Y), jnp.bfloat16),
                 field,
                 field,
                 crossing,
@@ -520,18 +568,18 @@
                 pltpu.VMEM((Q, R, Z, Y), f32),
                 pltpu.VMEM((Q, R, Z, Y), f32),
                 pltpu.VMEM((Q - 1, R, Z, Y), f32),
-                extended,
-                extended,
-                pltpu.VMEM((D, Z, Y), f32),
-                pltpu.VMEM((R, Z, Y), f32),
-                pltpu.VMEM((R, Z, Y), f32),
+                pltpu.VMEM((R + 4, Z + 2 * ZP, Y), f32),
+                pltpu.VMEM((R + 4, Z + 2 * ZP, Y), f32),
+                field,
+                pltpu.VMEM((D, 8, Y), f32),
+                pltpu.VMEM((S, 8, Y), f32),
                 dma((8,)),
-                dma((12,)),
-                dma((12,)),
+                dma((8,)),
+                dma((8,)),
                 dma((4 * O,)),
                 dma((4 * O,)),
-                dma((4 * O,)),
-                dma((4 * O,)),
+                dma((16,)),
+                dma((16,)),
                 dma((4 * O,)),
                 dma((4 * O,)),
                 dma,
@@ -540,10 +588,11 @@
                 dma((Q - 1,)),
                 dma((D - 1,)),
                 dma((D - 1,)),
-                dma((3,)),
+                dma((S - 1,)),
+                dma((S - 1,)),
             ],
             compiler_params=pltpu.CompilerParams(
-                collective_id=0, has_side_effects=True, vmem_limit_bytes=40 * 1024 * 1024
+                collective_id=0, has_side_effects=True, vmem_limit_bytes=56 * 1024 * 1024
             ),
         )(u_prev, u_cur, a_prev, a_cur, model, *rest)
 

time: 74.5 us -> 61.4 us (0.82)
  Pallas kernels: 61.9 us -> 53.7 us
  local copies, waits for them, and re-layouts: 10 us -> 5.24 us
    pallas_call x1, Pallas kernels: 61.9 us -> 53.7 us  [body(): pl.pallas_call(functools.partial(kernel, dims), out_shape=(jax.ShapeDtype...]
    unnamed x26 -> x6, local copies, waits for them, and re-layouts: 10 us -> 5.24 us
where the time goes in v2:
time: 61.4 us; the launch traced here: 60.9 us
  Pallas kernels  53.7 us (87%)
  local copies, waits for them, and re-layouts  5.24 us (9%)
  between operations  1.94 us (3%)
    pallas_call x1, Pallas kernels, body(): pl.pallas_call(functools.partial(kernel, dims), out_shape=(jax.ShapeDtype...  53.7 us
    unnamed x6, local copies, waits for them, and re-layouts  5.24 us

profile of v2, /device:TPU:0, one launch (start us, length us, event | category | flops | bytes accessed | tf_op | source)
XLA Modules:
  0.0 60.9 jit_solution(6339470226985593209)
XLA Ops:
  1.9 1.4 %copy.17.bins = s32[16,2,4]{2,1,0:T(2,128)} copy(s32[16,2,4]{0,2,1:T(4,128)} %param.22) | data formatting | bytes 1024 | tf_op args[8]
  3.3 53.7 %shard_map.157 = (f32[4,16,128]{2,1,0:T(8,128)}, f32[4,16,128]{2,1,0:T(8,128)}, f32[1,64,16,128]{3,2,1,0:T(8,128)}) custom-call(f32[1,64,16,128]{3,2,1,0:T(8,128)} %u_prev.1, f32[1,64,16,128]{3,2,1,0:T(8,128)} %u_cur.1, f32[1,64,16,128]{3,2,1,0:T(8,128)} %a_prev.1, f32[1,64,16,128]{3,2,1,0:T(8,128)} %a_cur.1, f32[4,16,128]{2,1,0:T(8,128)} %model.1, ...), custom_call_target="tpu_custom_call" | custom-call | tf_op jit(solution)/shard_map/pallas_call | solution.py:540
  57.0 0.0 copy-start
  57.0 1.4 %copy.23 = f32[4,16,128]{2,1,0:T(8,128)} copy(f32[4,16,128]{2,1,0:T(8,128)} %get-tuple-element.6) | data formatting | bytes 65536
  58.4 0.0 copy-done
  58.4 0.6 %copy.24 = f32[4,16,128]{2,1,0:T(8,128)} copy(f32[4,16,128]{2,1,0:T(8,128)S(1)} %copy-done) | data formatting | bytes 65536
  59.0 1.9 %copy.25 = f32[1,64,16,128]{3,2,1,0:T(8,128)} copy(f32[1,64,16,128]{3,2,1,0:T(8,128)} %get-tuple-element.8) | data formatting | bytes 1048576
Async XLA Ops:
  57.0 1.4 %copy-start = (f32[4,16,128]{2,1,0:T(8,128)S(1)}, f32[4,16,128]{2,1,0:T(8,128)}, u32[]{:S(2)}) copy-start(f32[4,16,128]{2,1,0:T(8,128)} %get-tuple-element.7) | copy-start | bytes 98308
